TPU v7x, 32 devices: a whole 2x2x4 slice. The times are simulated.
32 devices in a mesh: dp: 8 (over z, core), seq: 4 (over y, x).
Axes of the slice: x: 2, y: 2, z: 4, core: 2. Of those that a mesh axis runs over, the one named last changes fastest.
Arguments:
- tokens: bfloat16 [8, 1024, 1024], P('dp', 'seq'), may hold values from -6 to 6
- out_grad: bfloat16 [8, 1024, 1024], P('dp', 'seq'), may hold values from -6 to 6
- alibi_slopes: float32 [16], replicated, as said below
- qkv_weight: bfloat16 [1024, 3072], P(('dp', 'seq')), may hold values from -0.1875 to 0.1875
- dense_weight: bfloat16 [1024, 1024], P(('dp', 'seq')), may hold values from -0.75 to 0.75
- fc1_weight: bfloat16 [1024, 4096], P(('dp', 'seq')), may hold values from -0.1875 to 0.1875
- fc2_weight: bfloat16 [4096, 1024], P(('dp', 'seq')), may hold values from -0.09375 to 0.09375
- norm_gains: bfloat16 [2, 1024], P(None, ('dp', 'seq')), may hold values from 0.5 to 1.5
- biases: bfloat16 [6, 1024], P(None, ('dp', 'seq')), may hold values from -3 to 3
- fc1_bias: bfloat16 [4096], P(('dp', 'seq')), may hold values from -3 to 3
Outputs:
- layer_out: bfloat16 [8, 1024, 1024], P('dp', 'seq')
- tokens_grad: bfloat16 [8, 1024, 1024], P('dp', 'seq')
- qkv_grad: float32 [1024, 3072], P(('dp', 'seq'))
- dense_grad: float32 [1024, 1024], P(('dp', 'seq'))
- fc1_grad: float32 [1024, 4096], P(('dp', 'seq'))
- fc2_grad: float32 [4096, 1024], P(('dp', 'seq'))
- gains_grad: float32 [2, 1024], P(None, ('dp', 'seq'))
- biases_grad: float32 [6, 1024], P(None, ('dp', 'seq'))
- fc1_bias_grad: float32 [4096], P(('dp', 'seq'))
Inputs may be any that keep to these rules, and one draw needn't show every extreme that they name: `alibi_slopes`: each head's slope is positive, between 0.2 / 1024 and 0.1.
All inputs are finite; a program needn't handle non-finite values.
Results may differ from a plain program's by a relative error of at most 0.013.
Values may be sent and summed in bfloat16 or wider, within the bound.
A program may use at most 192 MiB of HBM per device.

v0:
```python
import jax
import jax.numpy as jnp
from jax import lax
from jax.sharding import PartitionSpec as P

HEADS = 16
HEAD_DIM = 64


epsilon = 1e-05
negative = -1e30


def layer_norm(values, gain_vec, shift_vec):
    row_mean = jnp.mean(values, axis=-1, keepdims=True)
    centred = values - row_mean
    spread = jnp.mean(centred * centred, axis=-1, keepdims=True)
    return centred * lax.rsqrt(spread + epsilon) * gain_vec + shift_vec


def gelu_tanh(values):
    return jax.nn.gelu(values, approximate=True)


def block_scores(query_blk, key_blk, slopes, q_start, k_start):
    scores = jnp.einsum(
        "qhe,khe->hqk", query_blk, key_blk, preferred_element_type=jnp.float32
    ) * HEAD_DIM ** (-0.5)
    grid_shape = (query_blk.shape[0], key_blk.shape[0])
    q_pos = q_start + lax.broadcasted_iota(jnp.int32, grid_shape, 0)
    k_pos = k_start + lax.broadcasted_iota(jnp.int32, grid_shape, 1)
    distance = (q_pos - k_pos).astype(jnp.float32)
    scores = scores - slopes[:, None, None] * distance[None]
    return jnp.where(distance[None] >= 0, scores, negative)


def block_grads(
    query_blk, key_blk, value_blk, grad_blk, lse_blk, delta_blk, slopes, q_start, k_start
):
    scores = block_scores(query_blk, key_blk, slopes, q_start, k_start)
    prob_vals = jnp.exp(scores - lse_blk[..., None])
    prob_low = prob_vals.astype(jnp.bfloat16)
    grad_probs = jnp.einsum("qhe,khe->hqk", grad_blk, value_blk, preferred_element_type=jnp.float32)
    grad_scores = (prob_vals * (grad_probs - delta_blk[..., None]) * HEAD_DIM ** (-0.5)).astype(
        jnp.bfloat16
    )
    grad_query = jnp.einsum(
        "hqk,khe->qhe", grad_scores, key_blk, preferred_element_type=jnp.float32
    )
    grad_key = jnp.einsum(
        "hqk,qhe->khe", grad_scores, query_blk, preferred_element_type=jnp.float32
    )
    grad_value = jnp.einsum("hqk,qhe->khe", prob_low, grad_blk, preferred_element_type=jnp.float32)
    return (grad_query, grad_key, grad_value)


def causal_forward(q_heads, k_heads, v_heads, slopes, q_start, used_blocks, key_block):
    rows = q_heads.shape[0]
    local_heads = q_heads.shape[1]

    def lse_step(blk_index, carry):
        run_max, run_sum = carry
        key_blk = lax.dynamic_slice_in_dim(k_heads, blk_index * key_block, key_block, 0)
        scores = block_scores(q_heads, key_blk, slopes, q_start, blk_index * key_block)
        new_max = jnp.maximum(run_max, jnp.max(scores, axis=-1))
        run_sum = run_sum * jnp.exp(run_max - new_max) + jnp.sum(
            jnp.exp(scores - new_max[..., None]), axis=-1
        )
        return (new_max, run_sum)

    start_max = jnp.full((local_heads, rows), negative, jnp.float32)
    run_max, run_sum = lax.fori_loop(
        0, used_blocks, lse_step, (start_max, jnp.zeros((local_heads, rows), jnp.float32))
    )
    log_total = run_max + jnp.log(run_sum)

    def out_step(blk_index, attended):
        key_blk = lax.dynamic_slice_in_dim(k_heads, blk_index * key_block, key_block, 0)
        value_blk = lax.dynamic_slice_in_dim(v_heads, blk_index * key_block, key_block, 0)
        scores = block_scores(q_heads, key_blk, slopes, q_start, blk_index * key_block)
        prob_low = jnp.exp(scores - log_total[..., None]).astype(jnp.bfloat16)
        return attended + jnp.einsum(
            "hqk,khe->qhe", prob_low, value_blk, preferred_element_type=jnp.float32
        )

    attended = lax.fori_loop(
        0, used_blocks, out_step, jnp.zeros((rows, local_heads, HEAD_DIM), jnp.float32)
    )
    return (attended, log_total)


def body(
    tokens,
    out_grad,
    alibi_slopes,
    qkv_weight,
    dense_weight,
    fc1_weight,
    fc2_weight,
    norm_gains,
    biases,
    fc1_bias,
):
    gathered = (
        lax.all_gather(qkv_weight, ("dp", "seq"), axis=0, tiled=True),
        lax.all_gather(dense_weight, ("dp", "seq"), axis=0, tiled=True),
        lax.all_gather(fc1_weight, ("dp", "seq"), axis=0, tiled=True),
        lax.all_gather(fc2_weight, ("dp", "seq"), axis=0, tiled=True),
        lax.all_gather(norm_gains, ("dp", "seq"), axis=1, tiled=True),
        lax.all_gather(biases, ("dp", "seq"), axis=1, tiled=True),
        lax.all_gather(fc1_bias, ("dp", "seq"), axis=0, tiled=True),
    )
    w_qkv, w_dense, w_fc1, w_fc2, gains_low, shifts_low, fc1_low = gathered
    gains = gains_low.astype(jnp.float32)
    shifts = shifts_low.astype(jnp.float32)
    fc1_shift = fc1_low.astype(jnp.float32)
    model_width = HEADS * HEAD_DIM
    tok_rows = tokens.shape[1]
    seq_length = tok_rows * lax.axis_size("seq")
    first_row = lax.axis_index("seq") * tok_rows
    key_block = min(512, tok_rows)
    inputs = tokens[0].astype(jnp.float32)
    normed_one, norm_pull_one = jax.vjp(layer_norm, inputs, gains[0], shifts[0])
    h_one = normed_one.astype(jnp.bfloat16)
    proj_bias = jnp.concatenate([shifts[1], jnp.zeros_like(shifts[1]), shifts[2]])
    projected = (jnp.dot(h_one, w_qkv, preferred_element_type=jnp.float32) + proj_bias).astype(
        jnp.bfloat16
    )
    query_rows = projected[:, :model_width]
    key_rows = projected[:, model_width : 2 * model_width]
    value_rows = projected[:, 2 * model_width :]
    q_heads = query_rows.reshape(tok_rows, HEADS, HEAD_DIM)
    key_all, value_all = (
        lax.all_gather(key_rows, "seq", axis=0, tiled=True),
        lax.all_gather(value_rows, "seq", axis=0, tiled=True),
    )
    k_heads = key_all.reshape(seq_length, HEADS, HEAD_DIM)
    v_heads = value_all.reshape(seq_length, HEADS, HEAD_DIM)
    used_blocks = (first_row + tok_rows) // key_block
    attended, log_total = causal_forward(
        q_heads, k_heads, v_heads, alibi_slopes, first_row, used_blocks, key_block
    )
    attended_low = attended.reshape(tok_rows, model_width).astype(jnp.bfloat16)
    residual = (
        inputs + jnp.dot(attended_low, w_dense, preferred_element_type=jnp.float32) + shifts[3]
    )
    normed_two, norm_pull_two = jax.vjp(layer_norm, residual, gains[1], shifts[4])
    h_two = normed_two.astype(jnp.bfloat16)
    upper = jnp.dot(h_two, w_fc1, preferred_element_type=jnp.float32) + fc1_shift
    activated, gelu_pull = jax.vjp(gelu_tanh, upper)
    act_low = activated.astype(jnp.bfloat16)
    layer_out = (
        residual + jnp.dot(act_low, w_fc2, preferred_element_type=jnp.float32) + shifts[5]
    ).astype(jnp.bfloat16)
    weights_back = (
        lax.all_gather(qkv_weight, ("dp", "seq"), axis=0, tiled=True),
        lax.all_gather(dense_weight, ("dp", "seq"), axis=0, tiled=True),
        lax.all_gather(fc1_weight, ("dp", "seq"), axis=0, tiled=True),
        lax.all_gather(fc2_weight, ("dp", "seq"), axis=0, tiled=True),
        lax.all_gather(norm_gains, ("dp", "seq"), axis=1, tiled=True),
        lax.all_gather(biases, ("dp", "seq"), axis=1, tiled=True),
        lax.all_gather(fc1_bias, ("dp", "seq"), axis=0, tiled=True),
    )
    back_qkv, back_dense, back_fc1, back_fc2 = (
        weights_back[0],
        weights_back[1],
        weights_back[2],
        weights_back[3],
    )
    cotangent = out_grad[0]
    grad_fc2_bias = jnp.sum(cotangent, axis=0, dtype=jnp.float32)
    grad_fc2 = jnp.einsum("tf,td->fd", act_low, cotangent, preferred_element_type=jnp.float32)
    grad_act = jnp.einsum("td,fd->tf", cotangent, back_fc2, preferred_element_type=jnp.float32)
    grad_upper = gelu_pull(grad_act)[0].astype(jnp.bfloat16)
    grad_fc1_bias = jnp.sum(grad_upper, axis=0, dtype=jnp.float32)
    grad_fc1 = jnp.einsum("td,tf->df", h_two, grad_upper, preferred_element_type=jnp.float32)
    grad_h_two = jnp.einsum("tf,df->td", grad_upper, back_fc1, preferred_element_type=jnp.float32)
    grad_res_norm, grad_gain_two, grad_shift_two = norm_pull_two(grad_h_two)
    grad_resid = cotangent.astype(jnp.float32) + grad_res_norm
    grad_branch = grad_resid.astype(jnp.bfloat16)
    grad_dense_bias = jnp.sum(grad_branch, axis=0, dtype=jnp.float32)
    grad_dense = jnp.einsum(
        "td,te->de", attended_low, grad_branch, preferred_element_type=jnp.float32
    )
    grad_attended = jnp.einsum(
        "te,de->td", grad_branch, back_dense, preferred_element_type=jnp.float32
    ).astype(jnp.bfloat16)
    g_heads = grad_attended.reshape(tok_rows, HEADS, HEAD_DIM)
    delta_rows = jnp.einsum("qhe,qhe->hq", g_heads.astype(jnp.float32), attended)

    def key_step(blk_index, carry):
        grad_q, grad_k_all, grad_v_all = carry
        key_blk = lax.dynamic_slice_in_dim(k_heads, blk_index * key_block, key_block, 0)
        value_blk = lax.dynamic_slice_in_dim(v_heads, blk_index * key_block, key_block, 0)
        part_q, part_k, part_v = block_grads(
            q_heads,
            key_blk,
            value_blk,
            g_heads,
            log_total,
            delta_rows,
            alibi_slopes,
            first_row,
            blk_index * key_block,
        )
        grad_k_all = lax.dynamic_update_slice_in_dim(
            grad_k_all, part_k.reshape(key_block, model_width), blk_index * key_block, 0
        )
        grad_v_all = lax.dynamic_update_slice_in_dim(
            grad_v_all, part_v.reshape(key_block, model_width), blk_index * key_block, 0
        )
        return (grad_q + part_q, grad_k_all, grad_v_all)

    start_state = (
        jnp.zeros((tok_rows, HEADS, HEAD_DIM), jnp.float32),
        jnp.zeros((seq_length, model_width), jnp.float32),
        jnp.zeros((seq_length, model_width), jnp.float32),
    )
    grad_q, grad_k_all, grad_v_all = lax.fori_loop(0, used_blocks, key_step, start_state)
    grad_keys, grad_values = (
        lax.psum_scatter(
            grad_k_all.astype(jnp.bfloat16), "seq", scatter_dimension=0, tiled=True
        ).astype(jnp.float32),
        lax.psum_scatter(
            grad_v_all.astype(jnp.bfloat16), "seq", scatter_dimension=0, tiled=True
        ).astype(jnp.float32),
    )
    grad_queries = grad_q.reshape(tok_rows, model_width)
    grad_proj = jnp.concatenate([grad_queries, grad_keys, grad_values], axis=1).astype(jnp.bfloat16)
    grad_query_bias = jnp.sum(grad_proj[:, :model_width], axis=0, dtype=jnp.float32)
    grad_value_bias = jnp.sum(grad_proj[:, 2 * model_width :], axis=0, dtype=jnp.float32)
    grad_qkv = jnp.einsum("td,tc->dc", h_one, grad_proj, preferred_element_type=jnp.float32)
    grad_h_one = jnp.einsum("tc,dc->td", grad_proj, back_qkv, preferred_element_type=jnp.float32)
    grad_in_norm, grad_gain_one, grad_shift_one = norm_pull_one(grad_h_one)
    tokens_grad = (grad_resid + grad_in_norm).astype(jnp.bfloat16)[None]
    gain_terms = jnp.stack([grad_gain_one, grad_gain_two])
    bias_terms = jnp.stack(
        [
            grad_shift_one,
            grad_query_bias,
            grad_value_bias,
            grad_dense_bias,
            grad_shift_two,
            grad_fc2_bias,
        ]
    )
    summed = (
        lax.psum_scatter(grad_qkv, ("dp", "seq"), scatter_dimension=0, tiled=True),
        lax.psum_scatter(grad_dense, ("dp", "seq"), scatter_dimension=0, tiled=True),
        lax.psum_scatter(grad_fc1, ("dp", "seq"), scatter_dimension=0, tiled=True),
        lax.psum_scatter(grad_fc2, ("dp", "seq"), scatter_dimension=0, tiled=True),
        lax.psum_scatter(gain_terms, ("dp", "seq"), scatter_dimension=1, tiled=True),
        lax.psum_scatter(bias_terms, ("dp", "seq"), scatter_dimension=1, tiled=True),
        lax.psum_scatter(grad_fc1_bias, ("dp", "seq"), scatter_dimension=0, tiled=True),
    )
    return (
        layer_out[None],
        tokens_grad,
        summed[0],
        summed[1],
        summed[2],
        summed[3],
        summed[4],
        summed[5],
        summed[6],
    )


def solution(mesh):
    return jax.shard_map(
        body,
        mesh=mesh,
        in_specs=(
            P("dp", "seq", None),
            P("dp", "seq", None),
            P(),
            P(("dp", "seq"), None),
            P(("dp", "seq"), None),
            P(("dp", "seq"), None),
            P(("dp", "seq"), None),
            P(None, ("dp", "seq")),
            P(None, ("dp", "seq")),
            P(("dp", "seq")),
        ),
        out_specs=(
            P("dp", "seq", None),
            P("dp", "seq", None),
            P(("dp", "seq"), None),
            P(("dp", "seq"), None),
            P(("dp", "seq"), None),
            P(("dp", "seq"), None),
            P(None, ("dp", "seq")),
            P(None, ("dp", "seq")),
            P(("dp", "seq")),
        ),
        check_vma=False,
    )
```

profile of v0, /device:TPU:0, one launch (start us, length us, event | category | flops | bytes accessed | tf_op | source)
XLA Modules:
  0.0 1879.4 jit_solution(2271878635147328993)
XLA Ops:
  8.0 71.2 %all-gather.1 = bf16[32,32,6]{1,2,0:T(8,128)(2,1)S(1)} all-gather(bf16[1,32,6]{1,2,0:T(8,128)(2,1)} %bitcast.258), channel_id=1, replica_groups=mesh['dp'=8,'seq'=4] {'dp','seq'}, dimensions={0}, use_global_device_ids=true | all-gather | bytes 12672 | tf_op jit(solution)/shard_map/all_gather | solution.py:110
  79.2 63.1 %all-gather = bf16[32,32,2]{1,2,0:T(2,128)(2,1)S(1)} all-gather(bf16[1,32,2]{1,2,0:T(2,128)(2,1)} %bitcast.259), channel_id=1, replica_groups=mesh['dp'=8,'seq'=4] {'dp','seq'}, dimensions={0}, use_global_device_ids=true | all-gather | bytes 4224 | tf_op jit(solution)/shard_map/all_gather | solution.py:109
  145.7 4.9 fusion.45
  154.3 65.2 %all-gather.2 = bf16[32,1,128]{2,1,0:T(2,128)(2,1)S(1)} all-gather(bf16[1,1,128]{2,1,0:T(2,128)(2,1)S(1)} %bitcast.260), channel_id=1, replica_groups=mesh['dp'=8,'seq'=4] {'dp','seq'}, dimensions={0}, use_global_device_ids=true | all-gather | bytes 8448 | tf_op jit(solution)/shard_map/all_gather | solution.py:111
  238.5 43.6 %all-gather.16.cloned.1.call-done = bf16[1024,1024]{1,0:T(8,128)(2,1)} async-done(((bf16[32,1024]{1,0:T(8,128)(2,1)}), bf16[1024,1024]{1,0:T(8,128)(2,1)}) %all-gather.16.cloned.1.call-update) | async-done | bytes 2097168 | tf_op jit(solution)/shard_map/all_gather | solution.py:106
  286.0 75.3 %all-gather.18.cloned.1.call-done = bf16[1024,4096]{1,0:T(8,128)(2,1)} async-done(((bf16[32,4096]{1,0:T(8,128)(2,1)}), bf16[1024,4096]{1,0:T(8,128)(2,1)}) %all-gather.18.cloned.1.call-update) | async-done | bytes 8388624 | tf_op jit(solution)/shard_map/all_gather | solution.py:107
  361.3 8.1 convolution_add_fusion
  369.4 70.8 %all-gather.20.cloned.1.call-done = bf16[4096,1024]{1,0:T(8,128)(2,1)} async-done(((bf16[128,1024]{1,0:T(8,128)(2,1)}), bf16[4096,1024]{1,0:T(8,128)(2,1)}) %all-gather.20.cloned.1.call-update) | async-done | bytes 8388624 | tf_op jit(solution)/shard_map/all_gather | solution.py:108
  440.2 7.9 convert_reduce_fusion
  462.6 10.3 while.38
  474.5 62.4 %reduce-scatter.13.cloned.1.call-done = bf16[256,1024]{0,1:T(8,128)(2,1)} async-done(((bf16[1024,1024]{0,1:T(8,128)(2,1)}), bf16[256,1024]{0,1:T(8,128)(2,1)}) %reduce-scatter.13.cloned.1.call-update) | async-done | bytes 524304 | tf_op jit(solution)/shard_map/reduce_scatter | solution.py:221
  537.0 38.5 %reduce-scatter.15.cloned.1.call-done = bf16[256,1024]{0,1:T(8,128)(2,1)} async-done(((bf16[1024,1024]{0,1:T(8,128)(2,1)}), bf16[256,1024]{0,1:T(8,128)(2,1)}) %reduce-scatter.15.cloned.1.call-update) | async-done | bytes 524304 | tf_op jit(solution)/shard_map/reduce_scatter | solution.py:224
  575.4 5.4 fusion.81
  591.3 6.5 fusion.64
  599.5 8.2 fusion.80
  608.7 10.7 fusion.67
  619.5 39.7 %all-reduce = f32[4096]{0:T(1024)S(1)} all-reduce(f32[4096]{0:T(1024)S(1)} %get-tuple-element.314), channel_id=10, replica_groups=mesh['dp'=8,'seq'=4] {'dp','seq'}, use_global_device_ids=true, to_apply=%region_33.34.clone | all-reduce | flops 4096 | bytes 32768
  659.7 8.2 fusion.54
  668.0 50.2 %reduce-scatter.25.cloned.1.call-done = f32[32,2]{1,0:T(8,128)} async-done(((f32[1024,2]{1,0:T(8,128)}), f32[32,2]{1,0:T(8,128)}) %reduce-scatter.25.cloned.1.call-update) | async-done | bytes 272
  719.5 130.6 %reduce-scatter.27.cloned.1.call-done = f32[32,6]{1,0:T(8,128)} async-done(((f32[1024,6]{1,0:T(8,128)}), f32[32,6]{1,0:T(8,128)}) %reduce-scatter.27.cloned.1.call-update) | async-done | bytes 784
  851.6 138.9 %reduce-scatter.19.cloned.1.call-done = f32[32,1024]{1,0:T(8,128)} async-done(((f32[1024,1024]{1,0:T(8,128)}), f32[32,1024]{1,0:T(8,128)}) %reduce-scatter.19.cloned.1.call-update) | async-done | bytes 131088 | tf_op jit(solution)/shard_map/reduce_scatter | solution.py:249
  990.4 160.4 %reduce-scatter.17.cloned.1.call-done = f32[32,3072]{1,0:T(8,128)} async-done(((f32[1024,3072]{1,0:T(8,128)}), f32[32,3072]{1,0:T(8,128)}) %reduce-scatter.17.cloned.1.call-update) | async-done | bytes 393232 | tf_op jit(solution)/shard_map/reduce_scatter | solution.py:248
  1150.8 359.7 %reduce-scatter.21.cloned.1.call-done = f32[32,4096]{1,0:T(8,128)} async-done(((f32[1024,4096]{1,0:T(8,128)}), f32[32,4096]{1,0:T(8,128)}) %reduce-scatter.21.cloned.1.call-update) | async-done | bytes 524304 | tf_op jit(solution)/shard_map/reduce_scatter | solution.py:250
  1510.5 361.9 %reduce-scatter.23.cloned.1.call-done = f32[128,1024]{1,0:T(8,128)} async-done(((f32[4096,1024]{1,0:T(8,128)}), f32[128,1024]{1,0:T(8,128)}) %reduce-scatter.23.cloned.1.call-update) | async-done | bytes 524304 | tf_op jit(solution)/shard_map/reduce_scatter | solution.py:251
  (150 shorter events, 80.3 us)
Async XLA Ops:
  7.2 138.5 %all-gather.10.cloned.1.call-start = ((), (), s32[]{:S(2)}) async-start(), calls=%async_computation.8 | async-start | bytes 6488064 | tf_op jit(solution)/shard_map/all_gather | solution.py:105
  7.9 211.8 %all-gather.14.cloned.1.call-start = ((), (), s32[]{:S(2)}) async-start(), calls=%async_computation.10 | async-start | bytes 2621440 | tf_op jit(solution)/shard_map/all_gather | solution.py:134
  151.7 71.3 %all-gather.12.cloned.1.call-start = ((), (), s32[]{:S(2)}) async-start(), calls=%async_computation.9 | async-start | bytes 2621440 | tf_op jit(solution)/shard_map/all_gather | solution.py:135
  152.4 129.7 %all-gather.16.cloned.1.call-start = ((), (), s32[]{:S(2)}) async-start(), calls=%async_computation.11 | async-start | bytes 2162688 | tf_op jit(solution)/shard_map/all_gather | solution.py:106
  153.0 208.3 %all-gather.18.cloned.1.call-start = ((), (), s32[]{:S(2)}) async-start(), calls=%async_computation.12 | async-start | bytes 8650752 | tf_op jit(solution)/shard_map/all_gather | solution.py:107
  153.6 286.6 %all-gather.20.cloned.1.call-start = ((), (), s32[]{:S(2)}) async-start(), calls=%async_computation.13 | async-start | bytes 8650752 | tf_op jit(solution)/shard_map/all_gather | solution.py:108
  154.2 382.8 %reduce-scatter.13.cloned.1.call-start = ((), (), s32[]{:S(2)}) async-start(), calls=%async_computation.14 | async-start | bytes 2621440 | tf_op jit(solution)/shard_map/reduce_scatter | solution.py:221
  219.6 7.4 copy-start.18
  231.0 51.1 %copy-start.1 = (bf16[1,256,1024]{2,1,0:T(8,128)(2,1)S(1)}, bf16[1,256,1024]{2,1,0:T(8,128)(2,1)}, u32[]{:S(2)}) copy-start(bf16[1,256,1024]{2,1,0:T(8,128)(2,1)} %param.16) | copy-start | bytes 1572868
  235.7 133.8 %copy-start = (bf16[1024,16,64]{0,2,1:T(8,128)(2,1)}, bf16[1024,16,64]{0,2,1:T(8,128)(2,1)S(1)}, u32[]{:S(2)}) copy-start(bf16[1024,16,64]{0,2,1:T(8,128)(2,1)S(1)} %get-tuple-element.669) | copy-start | bytes 6291460
  440.2 9.2 copy-start.3
  440.2 9.2 copy-start.21
  452.6 8.4 copy-start.4
  472.9 102.5 %reduce-scatter.15.cloned.1.call-start = ((), (), s32[]{:S(2)}) async-start(), calls=%async_computation.15 | async-start | bytes 2621440 | tf_op jit(solution)/shard_map/reduce_scatter | solution.py:224
  473.6 244.6 %reduce-scatter.25.cloned.1.call-start = ((), (), s32[]{:S(2)}) async-start(), calls=%async_computation.20 | async-start | bytes 540672
  575.4 6.0 copy-start.5
  575.4 6.0 copy-start.8
  580.8 5.5 copy-start.6
  583.8 266.4 %reduce-scatter.27.cloned.1.call-start = ((), (), s32[]{:S(2)}) async-start(), calls=%async_computation.21 | async-start | bytes 540672
  586.2 404.2 %reduce-scatter.19.cloned.1.call-start = ((), (), s32[]{:S(2)}) async-start(), calls=%async_computation.17 | async-start | bytes 4325376 | tf_op jit(solution)/shard_map/reduce_scatter | solution.py:249
  590.0 560.8 %reduce-scatter.17.cloned.1.call-start = ((), (), s32[]{:S(2)}) async-start(), calls=%async_computation.16 | async-start | bytes 12976128 | tf_op jit(solution)/shard_map/reduce_scatter | solution.py:248
  597.9 912.6 %reduce-scatter.21.cloned.1.call-start = ((), (), s32[]{:S(2)}) async-start(), calls=%async_computation.18 | async-start | bytes 17301504 | tf_op jit(solution)/shard_map/reduce_scatter | solution.py:250
  607.7 1264.7 %reduce-scatter.23.cloned.1.call-start = ((), (), s32[]{:S(2)}) async-start(), calls=%async_computation.19 | async-start | bytes 17301504 | tf_op jit(solution)/shard_map/reduce_scatter | solution.py:251
  619.5 40.3 %copy-start.19 = (f32[1,1024]{1,0:T(1,128)S(1)}, f32[1,1024]{1,0:T(1,128)}, u32[]{:S(2)}) copy-start(f32[1,1024]{1,0:T(1,128)} %get-tuple-element.303) | copy-start | bytes 12292
  (12 other events, 20.4 us)
Sparse Core Ops, SparseCore 0:
  10.9 72.0 all-gather.9
  151.8 33.3 all-gather.13
  187.7 35.3 all-gather.11
  225.8 56.3 all-gather.15
  284.9 76.3 all-gather.17
  364.1 76.1 all-gather.19
  473.0 63.9 reduce-scatter.12
  540.2 35.1 reduce-scatter.14
  583.9 134.2 reduce-scatter.24
  720.4 129.7 reduce-scatter.26
  853.0 137.3 reduce-scatter.18
  996.9 153.9 reduce-scatter.16
  1153.8 356.6 reduce-scatter.20
  1513.3 359.0 reduce-scatter.22
where the time goes:
time: 1890 us; the launch traced here: 1880 us
  waiting for transfers between devices  1500 us (79%)
  blocking collectives  239 us (13%)
  matrix products  84.6 us (4%)
  local copies, waits for them, and re-layouts  29.2 us (2%)
    reduce_scatter x1, waiting for transfers between devices, body(): lax.psum_scatter(grad_fc2, ('dp', 'seq'), scatter_dimension=0, tiled=True)  362 us
    reduce_scatter x1, waiting for transfers between devices, body(): lax.psum_scatter(grad_fc1, ('dp', 'seq'), scatter_dimension=0, tiled=True)  360 us
    unnamed x16, waiting for transfers between devices  185 us
    reduce_scatter x1, waiting for transfers between devices, body(): lax.psum_scatter(grad_qkv, ('dp', 'seq'), scatter_dimension=0, tiled=True)  160 us
    reduce_scatter x1, waiting for transfers between devices, body(): lax.psum_scatter(grad_dense, ('dp', 'seq'), scatter_dimension=0, tiled=True)  139 us
    all_gather x1, waiting for transfers between devices, body(): lax.all_gather(fc1_weight, ('dp', 'seq'), axis=0, tiled=True)  75.3 us
    all_gather x1, blocking collectives, body(): lax.all_gather(biases, ('dp', 'seq'), axis=1, tiled=True)  71.2 us
    all_gather x1, waiting for transfers between devices, body(): lax.all_gather(fc2_weight, ('dp', 'seq'), axis=0, tiled=True)  70.8 us
  transfers between devices with their start and end apart: 14, of which 12 were waited for; matrix products, arithmetic and copies ran while one was open for 4% of the time, Pallas kernels for 0%

commit v1 on v0

v1 whole, which is shorter than its diff:
```python
import jax
import jax.numpy as jnp
from jax import lax
from jax.sharding import PartitionSpec as P

HEADS = 16
HEAD_DIM = 64


epsilon = 1e-05
negative = -1e30
low = jnp.bfloat16
wide = jnp.float32


def layer_norm(values, gain_vec, shift_vec):
    row_mean = jnp.mean(values, axis=-1, keepdims=True)
    centred = values - row_mean
    spread = jnp.mean(centred * centred, axis=-1, keepdims=True)
    return centred * lax.rsqrt(spread + epsilon) * gain_vec + shift_vec


def gelu_tanh(values):
    return jax.nn.gelu(values, approximate=True)


def dot(spec, left, right):
    return jnp.einsum(spec, left, right, preferred_element_type=wide)


def gather_seq(rows):
    return lax.all_gather(rows, "seq", axis=0, tiled=True)


def scatter_seq(rows):
    return lax.psum_scatter(rows, "seq", scatter_dimension=0, tiled=True).astype(wide)


def swap_seq(chunks):
    return lax.all_to_all(chunks, "seq", split_axis=0, concat_axis=0, tiled=True)


def gather_dp(rows):
    return lax.all_gather(rows, "dp", axis=0, tiled=True)


def scatter_dp(rows):
    return lax.psum_scatter(rows, "dp", scatter_dimension=0, tiled=True)


def attention_forward(q_heads, k_heads, v_heads, slopes, block):
    length = q_heads.shape[1]
    kept, outs = [], []
    for start in range(0, length, block):
        end = start + block
        scores = dot("hqe,hke->hqk", q_heads[:, start:end], k_heads[:, :end]) * HEAD_DIM ** (-0.5)
        q_pos = start + lax.broadcasted_iota(jnp.int32, (block, end), 0)
        k_pos = lax.broadcasted_iota(jnp.int32, (block, end), 1)
        distance = (q_pos - k_pos).astype(wide)
        scores = scores - slopes[:, None, None] * distance[None]
        scores = jnp.where(distance[None] >= 0, scores, negative)
        weights = jnp.exp(scores - jnp.max(scores, axis=-1, keepdims=True))
        total = jnp.sum(weights, axis=-1, keepdims=True)
        probs = (weights * (1.0 / total)).astype(low)
        kept.append(probs)
        outs.append(dot("hqk,hke->hqe", probs, v_heads[:, :end]))
    return jnp.concatenate(outs, axis=1), kept


def attention_backward(q_heads, k_heads, v_heads, g_heads, delta, kept, block):
    length = q_heads.shape[1]
    grad_q = []
    grad_k = jnp.zeros(k_heads.shape, wide)
    grad_v = jnp.zeros(v_heads.shape, wide)
    for index, start in enumerate(range(0, length, block)):
        end = start + block
        probs = kept[index]
        g_blk = g_heads[:, start:end]
        q_blk = q_heads[:, start:end]
        grad_probs = dot("hqe,hke->hqk", g_blk, v_heads[:, :end])
        grad_scores = (
            probs.astype(wide) * (grad_probs - delta[:, start:end, None]) * HEAD_DIM ** (-0.5)
        ).astype(low)
        grad_q.append(dot("hqk,hke->hqe", grad_scores, k_heads[:, :end]))
        grad_k = grad_k.at[:, :end].add(dot("hqk,hqe->hke", grad_scores, q_blk))
        grad_v = grad_v.at[:, :end].add(dot("hqk,hqe->hke", probs, g_blk))
    return jnp.concatenate(grad_q, axis=1), grad_k, grad_v


def body(
    tokens,
    out_grad,
    alibi_slopes,
    qkv_weight,
    dense_weight,
    fc1_weight,
    fc2_weight,
    norm_gains,
    biases,
    fc1_bias,
):
    n_dp, n_seq = lax.axis_size("dp"), lax.axis_size("seq")
    parts = n_dp * n_seq
    my_dp, my_seq = lax.axis_index("dp"), lax.axis_index("seq")
    me = my_dp * n_seq + my_seq
    width = HEADS * HEAD_DIM
    rows, length = tokens.shape[1], tokens.shape[1] * n_seq
    local_heads = HEADS // n_seq
    cols = width // n_seq
    w_rows = qkv_weight.shape[0]
    ff_rows = fc2_weight.shape[0]
    units = ff_rows * n_dp
    block = min(256, length)
    spread = [(b, (b % n_dp) * n_seq + b // n_dp) for b in range(parts)]
    back = [(there, b) for b, there in spread]

    small = jnp.concatenate([norm_gains.reshape(-1), biases.reshape(-1), fc1_bias])
    small = lax.all_gather(small, ("dp", "seq"), axis=0, tiled=False)
    vec = small[:, : 8 * w_rows].reshape(parts, 8, w_rows).transpose(1, 0, 2).reshape(8, width)
    vec = vec.astype(wide)
    gains, shifts = vec[:2], vec[2:]
    ff_bias = small[:, 8 * w_rows :].reshape(n_dp, n_seq, ff_rows)
    ff_bias = lax.dynamic_index_in_dim(ff_bias, my_seq, 1, keepdims=False).reshape(units)
    ff_bias = ff_bias.astype(wide)

    part_qkv = qkv_weight.reshape(w_rows, 3, n_seq, cols).transpose(2, 0, 1, 3)
    part_qkv = swap_seq(part_qkv.reshape(n_seq, w_rows, 3 * cols))
    w_qkv = gather_dp(part_qkv.reshape(n_seq * w_rows, 3 * cols))
    w_dense = gather_dp(lax.ppermute(dense_weight, ("dp", "seq"), spread))
    part_fc1 = fc1_weight.reshape(w_rows, n_dp, n_seq, ff_rows).transpose(2, 0, 1, 3)
    part_fc1 = swap_seq(part_fc1.reshape(n_seq, w_rows, units))
    w_fc1 = gather_dp(part_fc1.reshape(n_seq * w_rows, units))
    w_fc2 = gather_dp(fc2_weight)

    inputs = tokens[0].astype(wide)
    normed_one, norm_pull_one = jax.vjp(layer_norm, inputs, gains[0], shifts[0])
    h_one = gather_seq(normed_one.astype(low))
    dy = out_grad[0]
    dy_all = gather_seq(dy)

    def my_cols(row):
        return lax.dynamic_slice_in_dim(row, my_seq * cols, cols, 0)

    proj_bias = jnp.concatenate([my_cols(shifts[1]), jnp.zeros((cols,), wide), my_cols(shifts[2])])
    projected = (dot("td,dc->tc", h_one, w_qkv) + proj_bias).astype(low)
    heads_first = projected.reshape(length, 3, local_heads, HEAD_DIM).transpose(1, 2, 0, 3)
    q_heads, k_heads, v_heads = heads_first[0], heads_first[1], heads_first[2]
    slopes = lax.dynamic_slice_in_dim(alibi_slopes, my_seq * local_heads, local_heads, 0)
    attended, kept = attention_forward(q_heads, k_heads, v_heads, slopes, block)
    attended_low = attended.astype(low).transpose(1, 0, 2).reshape(length, cols)
    branch = scatter_seq(dot("tc,cd->td", attended_low, w_dense).astype(low))
    residual = inputs + branch + shifts[3]
    normed_two, norm_pull_two = jax.vjp(layer_norm, residual, gains[1], shifts[4])
    h_two = gather_seq(normed_two.astype(low))
    upper = dot("td,df->tf", h_two, w_fc1) + ff_bias
    activated, gelu_pull = jax.vjp(gelu_tanh, upper)
    act_low = activated.astype(low)
    grad_act = dot("td,fd->tf", dy_all, w_fc2)
    grad_upper = gelu_pull(grad_act)[0].astype(low)
    grad_h_two = scatter_seq(dot("tf,df->td", grad_upper, w_fc1).astype(low))
    layer_out = (
        residual + scatter_seq(dot("tf,fd->td", act_low, w_fc2).astype(low)) + shifts[5]
    ).astype(low)
    grad_fc2 = scatter_dp(dot("tf,td->fd", act_low, dy_all).astype(low))
    grad_fc1 = scatter_dp(dot("td,tf->df", h_two, grad_upper).astype(low))
    grad_fc1_bias = jnp.sum(grad_upper, axis=0, dtype=wide)

    grad_res_norm, grad_gain_two, grad_shift_two = norm_pull_two(grad_h_two)
    grad_resid = dy.astype(wide) + grad_res_norm
    grad_branch = grad_resid.astype(low)
    branch_all = gather_seq(grad_branch)
    grad_dense = scatter_dp(dot("tc,td->cd", attended_low, branch_all).astype(low))
    grad_attended = dot("td,cd->tc", branch_all, w_dense).astype(low)
    g_heads = grad_attended.reshape(length, local_heads, HEAD_DIM).transpose(1, 0, 2)
    delta = jnp.sum(g_heads.astype(wide) * attended, axis=-1)
    grad_q, grad_k, grad_v = attention_backward(
        q_heads, k_heads, v_heads, g_heads, delta, kept, block
    )
    grad_proj = jnp.stack([grad_q, grad_k, grad_v]).astype(low)
    grad_proj = grad_proj.transpose(2, 0, 1, 3).reshape(length, 3 * cols)
    grad_h_one = scatter_seq(dot("tc,dc->td", grad_proj, w_qkv).astype(low))
    grad_qkv = scatter_dp(dot("td,tc->dc", h_one, grad_proj).astype(low))
    proj_sums = jnp.sum(grad_proj, axis=0, dtype=wide)

    def place(values):
        return lax.dynamic_update_slice_in_dim(jnp.zeros((width,), wide), values, my_seq * cols, 0)

    grad_in_norm, grad_gain_one, grad_shift_one = norm_pull_one(grad_h_one)
    tokens_grad = (grad_resid + grad_in_norm).astype(low)[None]
    ff_placed = lax.dynamic_update_slice_in_dim(
        jnp.zeros((n_dp, n_seq, ff_rows), wide),
        grad_fc1_bias.reshape(n_dp, 1, ff_rows),
        my_seq,
        1,
    )
    vec_sums = jnp.stack(
        [
            grad_gain_one,
            grad_gain_two,
            grad_shift_one,
            place(proj_sums[:cols]),
            place(proj_sums[2 * cols :]),
            jnp.sum(grad_branch, axis=0, dtype=wide),
            grad_shift_two,
            jnp.sum(dy, axis=0, dtype=wide),
        ]
    )
    sums = lax.psum(jnp.concatenate([vec_sums.reshape(-1), ff_placed.reshape(-1)]), ("dp", "seq"))
    vec_sums = lax.dynamic_slice_in_dim(sums[: 8 * width].reshape(8, width), me * w_rows, w_rows, 1)
    fc1_bias_grad = lax.dynamic_slice_in_dim(sums, 8 * width + me * ff_rows, ff_rows, 0)

    out_fc1 = swap_seq(grad_fc1.reshape(n_seq, w_rows, units))
    out_fc1 = out_fc1.reshape(n_seq, w_rows, n_dp, ff_rows).transpose(1, 2, 0, 3)
    out_qkv = swap_seq(grad_qkv.reshape(n_seq, w_rows, 3 * cols))
    out_qkv = out_qkv.reshape(n_seq, w_rows, 3, cols).transpose(1, 2, 0, 3)
    out_dense = lax.ppermute(grad_dense, ("dp", "seq"), back)
    return (
        layer_out[None],
        tokens_grad,
        out_qkv.reshape(w_rows, 3 * width).astype(wide),
        out_dense.astype(wide),
        out_fc1.reshape(w_rows, units * n_seq).astype(wide),
        grad_fc2.astype(wide),
        vec_sums[:2],
        vec_sums[2:],
        fc1_bias_grad,
    )


def solution(mesh):
    return jax.shard_map(
        body,
        mesh=mesh,
        in_specs=(
            P("dp", "seq", None),
            P("dp", "seq", None),
            P(),
            P(("dp", "seq"), None),
            P(("dp", "seq"), None),
            P(("dp", "seq"), None),
            P(("dp", "seq"), None),
            P(None, ("dp", "seq")),
            P(None, ("dp", "seq")),
            P(("dp", "seq")),
        ),
        out_specs=(
            P("dp", "seq", None),
            P("dp", "seq", None),
            P(("dp", "seq"), None),
            P(("dp", "seq"), None),
            P(("dp", "seq"), None),
            P(("dp", "seq"), None),
            P(None, ("dp", "seq")),
            P(None, ("dp", "seq")),
            P(("dp", "seq")),
        ),
        check_vma=False,
    )
```

time: 1890 us -> 696 us (0.37)
  waiting for transfers between devices: 1500 us -> 382 us
  blocking collectives: 239 us -> 141 us
    reduce_scatter x6 -> x8, waiting for transfers between devices: 1120 us -> 227 us  [the longest x4 121 us: scatter_seq(): lax.psum_scatter(rows, 'seq', scatter_dimension=0, tiled=True).astype(wide)]
    unnamed x16 -> x15, waiting for transfers between devices: 185 us -> 1.43 us
    all_gather x3 -> x2, blocking collectives: 199 us -> 80.5 us  [the longest x1 65.4 us: body(): small = lax.all_gather(small, ('dp', 'seq'), axis=0, tiled=False)]
    psum x0 -> x1, blocking collectives: none -> 39.8 us  [body(): lax.psum(jnp.concatenate([vec_sums.reshape(-1), ff_placed.reshape(-1)]),...]
    unnamed x1 -> x0, blocking collectives: 39.7 us -> none
    all_gather x6 -> x7, waiting for transfers between devices: 190 us -> 154 us  [the longest x4 98.8 us: gather_seq(): return lax.all_gather(rows, 'seq', axis=0, tiled=True)]
    all_to_all x0 -> x2, blocking collectives: none -> 21.1 us  [swap_seq(): lax.all_to_all(chunks, 'seq', split_axis=0, concat_axis=0, tiled=True)]
    dot_general x19 -> x32, matrix products: 84.6 us -> 70.9 us  [dot(): return jnp.einsum(spec, left, right, preferred_element_type=wide)]
  transfers between devices with their start and end apart: 14 -> 19, of which waited for: 12 -> 14; matrix products, arithmetic and copies ran while one was open for 4% -> 10% of each run, Pallas kernels for 0% -> 0%
where the time goes in v1:
time: 696 us; the launch traced here: 692 us
  waiting for transfers between devices  382 us (55%)
  blocking collectives  141 us (20%)
  matrix products  87.4 us (13%)
  other arithmetic  31.6 us (5%)
  local copies, waits for them, and re-layouts  23.8 us (3%)
  between operations  14.8 us (2%)
  starting transfers between devices  10.6 us (2%)
    reduce_scatter x4, waiting for transfers between devices, scatter_seq(): lax.psum_scatter(rows, 'seq', scatter_dimension=0, tiled=True).astype(wide)  121 us
    reduce_scatter x4, waiting for transfers between devices, scatter_dp(): return lax.psum_scatter(rows, 'dp', scatter_dimension=0, tiled=True)  106 us
    all_gather x4, waiting for transfers between devices, gather_seq(): return lax.all_gather(rows, 'seq', axis=0, tiled=True)  98.8 us
    dot_general x32, matrix products, dot(): return jnp.einsum(spec, left, right, preferred_element_type=wide)  70.9 us
    all_gather x1, blocking collectives, body(): small = lax.all_gather(small, ('dp', 'seq'), axis=0, tiled=False)  65.4 us
    all_gather x3, waiting for transfers between devices, gather_dp(): return lax.all_gather(rows, 'dp', axis=0, tiled=True)  55.1 us
    psum x1, blocking collectives, body(): lax.psum(jnp.concatenate([vec_sums.reshape(-1), ff_placed.reshape(-1)]),...  39.8 us
    all_to_all x2, blocking collectives, swap_seq(): lax.all_to_all(chunks, 'seq', split_axis=0, concat_axis=0, tiled=True)  21.1 us
  transfers between devices with their start and end apart: 19, of which 14 were waited for; matrix products, arithmetic and copies ran while one was open for 10% of the time, Pallas kernels for 0%

profile of v1, /device:TPU:0, one launch (start us, length us, event | category | flops | bytes accessed | tf_op | source)
XLA Modules:
  0.0 691.9 jit_solution(5945987798339886245)
XLA Ops:
  8.7 10.6 %all_to_all.20 = bf16[4,32,768]{2,1,0:T(8,128)(2,1)} all-to-all(bf16[4,32,768]{2,1,0:T(8,128)(2,1)S(1)} %reshape.561), channel_id=1, replica_groups=mesh['dp'=8,'seq'=4] {'seq'}, dimensions={0} | all-to-all | bytes 393216 | tf_op jit(solution)/shard_map/all_to_all | solution.py:40
  21.6 65.4 %all-gather.2 = bf16[32,1,384]{2,1,0:T(2,128)(2,1)S(1)} all-gather(bf16[1,1,384]{2,1,0:T(2,128)(2,1)S(1)} %reshape.589), channel_id=2, replica_groups=mesh['dp'=8,'seq'=4] {'dp','seq'}, dimensions={0}, use_global_device_ids=true | all-gather | bytes 25344 | tf_op jit(solution)/shard_map/all_gather | solution.py:118
  97.7 15.1 %all_gather.34 = bf16[256,1024]{1,0:T(8,128)(2,1)S(1)} all-gather(bf16[32,1024]{1,0:T(8,128)(2,1)S(1)} %collective-permute-done), channel_id=1, replica_groups=mesh['dp'=8,'seq'=4] {'dp'}, dimensions={0}, use_global_device_ids=true | all-gather | bytes 589824 | tf_op jit(solution)/shard_map/all_gather | solution.py:44
  112.8 9.3 %all-gather.11.cloned.1.call-done = bf16[1024,1024]{1,0:T(8,128)(2,1)} async-done(((bf16[256,1024]{1,0:T(8,128)(2,1)}), bf16[1024,1024]{1,0:T(8,128)(2,1)}) %all-gather.11.cloned.1.call-update) | async-done | bytes 2097168 | tf_op jit(solution)/shard_map/all_gather | solution.py:32
  163.2 10.4 %all_to_all.21 = bf16[4,32,1024]{2,1,0:T(8,128)(2,1)} all-to-all(bf16[4,32,1024]{2,1,0:T(8,128)(2,1)S(1)} %reshape.566), channel_id=1, replica_groups=mesh['dp'=8,'seq'=4] {'seq'}, dimensions={0} | all-to-all | bytes 524288 | tf_op jit(solution)/shard_map/all_to_all | solution.py:40
  173.9 24.3 %reduce-scatter.9.cloned.1.call-done = bf16[256,1024]{1,0:T(8,128)(2,1)} async-done(((bf16[1024,1024]{1,0:T(8,128)(2,1)}), bf16[256,1024]{1,0:T(8,128)(2,1)}) %reduce-scatter.9.cloned.1.call-update) | async-done | bytes 524304 | tf_op jit(solution)/shard_map/reduce_scatter | solution.py:36
  204.6 24.3 %all-gather.17.cloned.1.call-done = bf16[1024,1024]{1,0:T(8,128)(2,1)} async-done(((bf16[128,1024]{1,0:T(8,128)(2,1)}), bf16[1024,1024]{1,0:T(8,128)(2,1)}) %all-gather.17.cloned.1.call-update) | async-done | bytes 2097168 | tf_op jit(solution)/shard_map/all_gather | solution.py:44
  228.9 37.3 %all-gather.15.cloned.1.call-done = bf16[1024,1024]{1,0:T(8,128)(2,1)} async-done(((bf16[256,1024]{1,0:T(8,128)(2,1)}), bf16[1024,1024]{1,0:T(8,128)(2,1)}) %all-gather.15.cloned.1.call-update) | async-done | bytes 2097168 | tf_op jit(solution)/shard_map/all_gather | solution.py:32
  266.2 6.5 fusion.173
  272.6 30.7 %all-gather.23.cloned.1.call-done = bf16[1,1024,1024]{2,1,0:T(8,128)(2,1)} async-done(((bf16[1,256,1024]{2,1,0:T(8,128)(2,1)}), bf16[1,1024,1024]{2,1,0:T(8,128)(2,1)}) %all-gather.23.cloned.1.call-update) | async-done | bytes 2097168 | tf_op jit(solution)/shard_map/all_gather | solution.py:32
  303.4 30.8 %all-gather.19.cloned.1.call-done = bf16[1024,1024]{1,0:T(8,128)(2,1)} async-done(((bf16[128,1024]{1,0:T(8,128)(2,1)}), bf16[1024,1024]{1,0:T(8,128)(2,1)}) %all-gather.19.cloned.1.call-update) | async-done | bytes 2097168 | tf_op jit(solution)/shard_map/all_gather | solution.py:44
  334.2 8.4 %convert_reduce_fusion = (f32[1024]{0:T(1024)S(1)}, bf16[1024,1024]{1,0:T(8,128)(2,1)S(1)}) fusion(f32[1024,1024]{1,0:T(8,128)} %fusion.173, f32[1024]{0:T(1024)S(1)} %bitcast.235, bf16[1024,1024]{1,0:T(8,128)(2,1)} %all-gather.19.cloned.1.call-done, bf16[1,1024,1024]{2,1,0:T(8,128)(2,1)} %all-gather.23.cloned.1.call-done), kind=kOutput, calls=%fused_computation.13 | convolution fusion | flops 2171599872 | bytes 10493952 | tf_op jit(solution)/shard_map/td,fd->tf/dot_general | solution.py:28
  347.7 7.0 %convolution_convert_fusion.2 = bf16[1024,1024]{1,0:T(8,128)(2,1)} fusion(bf16[1024,1024]{1,0:T(8,128)(2,1)} %all-gather.19.cloned.1.call-done, f32[1024,1024]{1,0:T(8,128)} %fusion.173, f32[1024]{0:T(1024)S(1)} %bitcast.236), kind=kOutput, calls=%fused_computation.43 | convolution fusion | flops 2159017984 | bytes 8392704 | tf_op jit(solution)/shard_map/tf,fd->td/dot_general | solution.py:28
  355.5 27.0 %reduce-scatter.13.cloned.1.call-done = bf16[256,1024]{1,0:T(8,128)(2,1)} async-done(((bf16[1024,1024]{1,0:T(8,128)(2,1)}), bf16[256,1024]{1,0:T(8,128)(2,1)}) %reduce-scatter.13.cloned.1.call-update) | async-done | bytes 524304 | tf_op jit(solution)/shard_map/reduce_scatter | solution.py:36
  384.1 36.6 %reduce-scatter.11.cloned.1.call-done = bf16[256,1024]{1,0:T(8,128)(2,1)} async-done(((bf16[1024,1024]{1,0:T(8,128)(2,1)}), bf16[256,1024]{1,0:T(8,128)(2,1)}) %reduce-scatter.11.cloned.1.call-update) | async-done | bytes 524304 | tf_op jit(solution)/shard_map/reduce_scatter | solution.py:36
  425.4 6.0 convolution_convert_fusion
  431.4 7.6 %fusion.24 = bf16[1024,1024]{1,0:T(8,128)(2,1)} fusion(bf16[1,1024,1024]{2,1,0:T(8,128)(2,1)} %all-gather.23.cloned.1.call-done, f32[1024,1024]{1,0:T(8,128)} %fusion.173, f32[1024]{0:T(1024)S(1)} %bitcast.237), kind=kOutput, calls=%fused_computation.40 | convolution fusion | flops 2159017984 | bytes 8392704 | tf_op jit(solution)/shard_map/tf,td->fd/dot_general | solution.py:28
  439.3 21.5 %all-gather.21.cloned.1.call-done = bf16[1024,1024]{1,0:T(8,128)(2,1)} async-done(((bf16[256,1024]{1,0:T(8,128)(2,1)}), bf16[1024,1024]{1,0:T(8,128)(2,1)}) %all-gather.21.cloned.1.call-update) | async-done | bytes 2097168 | tf_op jit(solution)/shard_map/all_gather | solution.py:32
  485.5 13.6 %reduce-scatter.21.cloned.1.call-done = bf16[128,1024]{1,0:T(8,128)(2,1)} async-done(((bf16[1024,1024]{1,0:T(8,128)(2,1)}), bf16[128,1024]{1,0:T(8,128)(2,1)}) %reduce-scatter.21.cloned.1.call-update) | async-done | bytes 262160 | tf_op jit(solution)/shard_map/reduce_scatter | solution.py:48
  502.9 32.9 %reduce-scatter.23.cloned.1.call-done = bf16[128,1024]{1,0:T(8,128)(2,1)} async-done(((bf16[1024,1024]{1,0:T(8,128)(2,1)}), bf16[128,1024]{1,0:T(8,128)(2,1)}) %reduce-scatter.23.cloned.1.call-update) | async-done | bytes 262160 | tf_op jit(solution)/shard_map/reduce_scatter | solution.py:48
  539.0 32.0 %reduce-scatter.17.cloned.1.call-done = bf16[128,768]{1,0:T(8,128)(2,1)} async-done(((bf16[1024,768]{1,0:T(8,128)(2,1)}), bf16[128,768]{1,0:T(8,128)(2,1)}) %reduce-scatter.17.cloned.1.call-update) | async-done | bytes 196624 | tf_op jit(solution)/shard_map/reduce_scatter | solution.py:48
  574.8 28.0 %reduce-scatter.19.cloned.1.call-done = bf16[32,1024]{1,0:T(8,128)(2,1)} async-done(((bf16[256,1024]{1,0:T(8,128)(2,1)}), bf16[32,1024]{1,0:T(8,128)(2,1)}) %reduce-scatter.19.cloned.1.call-update) | async-done | bytes 65552 | tf_op jit(solution)/shard_map/reduce_scatter | solution.py:48
  606.4 32.6 %reduce-scatter.15.cloned.1.call-done = bf16[256,1024]{1,0:T(8,128)(2,1)} async-done(((bf16[1024,1024]{1,0:T(8,128)(2,1)}), bf16[256,1024]{1,0:T(8,128)(2,1)}) %reduce-scatter.15.cloned.1.call-update) | async-done | bytes 524304 | tf_op jit(solution)/shard_map/reduce_scatter | solution.py:36
  642.2 39.8 %psum.7 = f32[12288]{0:T(1024)S(1)} all-reduce(f32[12288]{0:T(1024)S(1)} %pad_maximum_fusion.2), channel_id=1, replica_groups=mesh['dp'=8,'seq'=4] {'dp','seq'}, use_global_device_ids=true, to_apply=%region_33.34 | all-reduce | flops 12288 | bytes 98304 | tf_op jit(solution)/shard_map/psum | solution.py:208
  (247 shorter events, 119.3 us)
Async XLA Ops:
  7.2 81.6 %copy-start = (bf16[1,256,1024]{2,1,0:T(8,128)(2,1)S(1)}, bf16[1,256,1024]{2,1,0:T(8,128)(2,1)}, u32[]{:S(2)}) copy-start(bf16[1,256,1024]{2,1,0:T(8,128)(2,1)} %param.30) | copy-start | bytes 1572868
  7.2 105.6 %all-gather.13.cloned.1.call-start = ((), (), s32[]{:S(2)}) async-start(), calls=%async_computation.13 | async-start | bytes 1769472 | tf_op jit(solution)/shard_map/all_gather | solution.py:44
  8.5 81.9 %copy-start.34 = (bf16[32,1024]{1,0:T(8,128)(2,1)S(1)}, bf16[32,1024]{1,0:T(8,128)(2,1)}, u32[]{:S(2)}) copy-start(bf16[32,1024]{1,0:T(8,128)(2,1)} %param.34) | copy-start | bytes 196612
  8.5 82.7 %copy-start.35 = (f32[16]{0:T(128)S(1)}, f32[16]{0:T(128)}, u32[]{:S(2)}) copy-start(f32[16]{0:T(128)} %param.32) | copy-start | bytes 196
  19.3 102.7 %all-gather.11.cloned.1.call-start = ((), (), s32[]{:S(2)}) async-start(), calls=%async_computation.12 | async-start | bytes 2621440 | tf_op jit(solution)/shard_map/all_gather | solution.py:32
  90.3 107.9 %reduce-scatter.9.cloned.1.call-start = ((), (), s32[]{:S(2)}) async-start(), calls=%async_computation.14 | async-start | bytes 2621440 | tf_op jit(solution)/shard_map/reduce_scatter | solution.py:36
  90.4 7.3 %collective-permute-start = (bf16[32,1024]{1,0:T(8,128)(2,1)S(1)}, bf16[32,1024]{1,0:T(8,128)(2,1)S(1)}, u32[]{:S(2)}, u32[]{:S(2)}) collective-permute-start(bf16[32,1024]{1,0:T(8,128)(2,1)S(1)} %copy-done.34), channel_id=1, source_target_pairs={{0,0},{1,4},{2,8},{3,12},{4,16},{5,20},{6,24},{7,28},{8,1},{9,5},{... | collective-permute-start | bytes 196616 | tf_op jit(solution)/shard_map/ppermute | solution.py:129
  112.7 46.3 %copy-start.20 = (bf16[256,1024]{1,0:T(8,128)(2,1)}, bf16[256,1024]{1,0:T(8,128)(2,1)S(1)}, u32[]{:S(2)}) copy-start(bf16[256,1024]{1,0:T(8,128)(2,1)S(1)} %all_gather.34) | copy-start | bytes 1572868
  161.9 67.0 %all-gather.17.cloned.1.call-start = ((), (), s32[]{:S(2)}) async-start(), calls=%async_computation.16 | async-start | bytes 2359296 | tf_op jit(solution)/shard_map/all_gather | solution.py:44
  173.6 92.5 %all-gather.15.cloned.1.call-start = ((), (), s32[]{:S(2)}) async-start(), calls=%async_computation.15 | async-start | bytes 2621440 | tf_op jit(solution)/shard_map/all_gather | solution.py:32
  202.1 101.2 %all-gather.23.cloned.1.call-start = ((), (), s32[]{:S(2)}) async-start(), calls=%async_computation.26 | async-start | bytes 2621440 | tf_op jit(solution)/shard_map/all_gather | solution.py:32
  202.7 131.5 %all-gather.19.cloned.1.call-start = ((), (), s32[]{:S(2)}) async-start(), calls=%async_computation.17 | async-start | bytes 2359296 | tf_op jit(solution)/shard_map/all_gather | solution.py:44
  203.5 179.1 %reduce-scatter.13.cloned.1.call-start = ((), (), s32[]{:S(2)}) async-start(), calls=%async_computation.19 | async-start | bytes 2621440 | tf_op jit(solution)/shard_map/reduce_scatter | solution.py:36
  347.6 73.1 %reduce-scatter.11.cloned.1.call-start = ((), (), s32[]{:S(2)}) async-start(), calls=%async_computation.18 | async-start | bytes 2621440 | tf_op jit(solution)/shard_map/reduce_scatter | solution.py:36
  354.7 106.1 %all-gather.21.cloned.1.call-start = ((), (), s32[]{:S(2)}) async-start(), calls=%async_computation.20 | async-start | bytes 2621440 | tf_op jit(solution)/shard_map/all_gather | solution.py:32
  425.4 73.7 %reduce-scatter.21.cloned.1.call-start = ((), (), s32[]{:S(2)}) async-start(), calls=%async_computation.24 | async-start | bytes 2359296 | tf_op jit(solution)/shard_map/reduce_scatter | solution.py:48
  431.4 104.4 %reduce-scatter.23.cloned.1.call-start = ((), (), s32[]{:S(2)}) async-start(), calls=%async_computation.25 | async-start | bytes 2359296 | tf_op jit(solution)/shard_map/reduce_scatter | solution.py:48
  439.1 132.0 %reduce-scatter.17.cloned.1.call-start = ((), (), s32[]{:S(2)}) async-start(), calls=%async_computation.22 | async-start | bytes 1769472 | tf_op jit(solution)/shard_map/reduce_scatter | solution.py:48
  477.5 125.2 %reduce-scatter.19.cloned.1.call-start = ((), (), s32[]{:S(2)}) async-start(), calls=%async_computation.23 | async-start | bytes 589824 | tf_op jit(solution)/shard_map/reduce_scatter | solution.py:48
  480.7 158.2 %reduce-scatter.15.cloned.1.call-start = ((), (), s32[]{:S(2)}) async-start(), calls=%async_computation.21 | async-start | bytes 2621440 | tf_op jit(solution)/shard_map/reduce_scatter | solution.py:36
  499.1 38.5 %all-to-all-start.3 = ((bf16[4,32,1024]{2,1,0:T(8,128)(2,1)}), bf16[4,32,1024]{2,1,0:T(8,128)(2,1)S(1)}, u32[]{:S(2)}, u32[]{:S(2)}) async-start(bf16[4,32,1024]{2,1,0:T(8,128)(2,1)} %bitcast.220), calls=%async_computation.10 | async-start | bytes 524288 | tf_op jit(solution)/shard_map/all_to_all | solution.py:40
  571.1 33.9 %all-to-all-start.2 = ((bf16[4,32,768]{2,1,0:T(8,128)(2,1)}), bf16[4,32,768]{2,1,0:T(8,128)(2,1)S(1)}, u32[]{:S(2)}, u32[]{:S(2)}) async-start(bf16[4,32,768]{2,1,0:T(8,128)(2,1)} %bitcast.221), calls=%async_computation.7 | async-start | bytes 393216 | tf_op jit(solution)/shard_map/all_to_all | solution.py:40
  602.8 1.5 collective-permute-start.1
  605.1 78.7 %copy-start.5 = (f32[256,1024]{1,0:T(8,128)S(1)}, f32[256,1024]{1,0:T(8,128)}, u32[]{:S(2)}) copy-start(f32[256,1024]{1,0:T(8,128)} %copy-done.4) | copy-start | bytes 3145732
  (33 other events, 212.0 us)
Sparse Core Ops, SparseCore 0:
  19.5 24.6 all-gather.12
  90.4 31.6 all-gather.10
  162.0 36.1 reduce-scatter.8
  199.8 29.0 all-gather.16
  231.3 34.7 all-gather.14
  268.0 35.2 all-gather.22
  305.0 29.0 all-gather.18
  347.7 34.7 reduce-scatter.12
  385.5 35.1 reduce-scatter.10
  425.5 35.2 all-gather.20
  463.2 35.7 reduce-scatter.20
  501.3 34.4 reduce-scatter.22
  538.2 32.8 reduce-scatter.16
  573.8 28.8 reduce-scatter.18
  605.6 33.3 reduce-scatter.14

commit v2 on v1

--- a/solution.py
+++ b/solution.py
@@ -1,6 +1,9 @@
+import functools
 import jax
 import jax.numpy as jnp
 from jax import lax
+from jax.experimental import pallas as pl
+from jax.experimental.pallas import tpu as pltpu
 from jax.sharding import PartitionSpec as P
 
 HEADS = 16
@@ -28,11 +31,208 @@
     return jnp.einsum(spec, left, right, preferred_element_type=wide)
 
 
-def gather_seq(rows):
-    return lax.all_gather(rows, "seq", axis=0, tiled=True)
-
-
-def scatter_seq(rows):
+def start_all(copies):
+    for copy in copies:
+        copy.start()
+
+
+def greet(targets):
+    barrier = pltpu.get_barrier_semaphore()
+    for target in targets:
+        pl.semaphore_signal(barrier, inc=1, device_id=target, device_id_type=pl.DeviceIdType.MESH)
+    pl.semaphore_wait(barrier, len(targets))
+
+
+def send(src, dst, send_sem, recv_sem, target):
+    return pltpu.make_async_remote_copy(
+        src_ref=src,
+        dst_ref=dst,
+        send_sem=send_sem,
+        recv_sem=recv_sem,
+        device_id=target,
+        device_id_type=pl.DeviceIdType.MESH,
+    )
+
+
+def exchange_kernel(count, is_gather, src, out, send_sem, recv_sem, local_sem):
+    mine, my_dp = lax.axis_index("seq"), lax.axis_index("dp")
+    peers = [lax.rem(mine + step, count) for step in range(1, count)]
+    greet([(my_dp, peer) for peer in peers])
+    copies = [
+        send(
+            src if is_gather else src.at[peer],
+            out.at[mine],
+            send_sem.at[step],
+            recv_sem.at[step],
+            (my_dp, peer),
+        )
+        for step, peer in enumerate(peers)
+    ]
+    start_all(copies)
+    local = pltpu.make_async_copy(src if is_gather else src.at[mine], out.at[mine], local_sem)
+    local.start()
+    local.wait()
+    for copy in copies:
+        copy.wait()
+
+
+def exchange(values, number, is_gather):
+    count = lax.axis_size("seq")
+    shape = (count, *values.shape) if is_gather else values.shape
+    return pl.pallas_call(
+        functools.partial(exchange_kernel, count, is_gather),
+        out_shape=jax.ShapeDtypeStruct(shape, values.dtype),
+        in_specs=[pl.BlockSpec(memory_space=pl.ANY)],
+        out_specs=pl.BlockSpec(memory_space=pl.ANY),
+        scratch_shapes=[
+            pltpu.SemaphoreType.DMA((count - 1,)),
+            pltpu.SemaphoreType.DMA((count - 1,)),
+            pltpu.SemaphoreType.DMA,
+        ],
+        compiler_params=pltpu.CompilerParams(collective_id=number, has_side_effects=True),
+        cost_estimate=pl.CostEstimate(flops=0, bytes_accessed=60_000_000, transcendentals=0),
+        name=f"exchange_{number}",
+    )(values)
+
+
+def open_kernel(
+    n_z, n_seq, x, dy, up, down, x_all, dy_all, up_all, down_all,
+    swap_s, swap_r, x_s, x_r, dy_s, dy_r, up_s, up_r, down_s, down_r, up_ts, up_tr, down_ts, down_tr,
+    local_sem,
+):
+    my_dp, my_seq = lax.axis_index("dp"), lax.axis_index("seq")
+    my_z, core = my_dp // 2, lax.rem(my_dp, 2)
+    seq_peers = [lax.rem(my_seq + step, n_seq) for step in range(1, n_seq)]
+    z_peers = [(lax.rem(my_z + step, n_z) * 2 + core, my_seq) for step in range(1, n_z)]
+    twin = (my_z * 2 + 1 - core, my_seq)
+    greet([(my_dp, peer) for peer in seq_peers] + z_peers + [twin])
+    swaps = [
+        send(up.at[p], up_all.at[my_dp, my_seq], swap_s.at[k], swap_r.at[k], (my_dp, p))
+        for k, p in enumerate(seq_peers)
+    ]
+    start_all(swaps)
+    downs = [
+        send(down, down_all.at[my_dp], down_s.at[k], down_r.at[k], target)
+        for k, target in enumerate(z_peers)
+    ]
+    start_all(downs)
+    down_twins = [send(down, down_all.at[my_dp], down_ts.at[0], down_tr.at[0], twin)]
+    start_all(down_twins)
+    rows = []
+    for k, p in enumerate(seq_peers):
+        rows.append(send(x, x_all.at[my_seq], x_s.at[k], x_r.at[k], (my_dp, p)))
+        rows.append(send(dy, dy_all.at[my_seq], dy_s.at[k], dy_r.at[k], (my_dp, p)))
+    start_all(rows)
+    own = [
+        pltpu.make_async_copy(up.at[my_seq], up_all.at[my_dp, my_seq], local_sem.at[0]),
+        pltpu.make_async_copy(down, down_all.at[my_dp], local_sem.at[1]),
+        pltpu.make_async_copy(x, x_all.at[my_seq], local_sem.at[2]),
+        pltpu.make_async_copy(dy, dy_all.at[my_seq], local_sem.at[3]),
+    ]
+    start_all(own)
+    for copy in own:
+        copy.wait()
+    for copy in swaps:
+        copy.wait()
+    ups = [
+        send(up_all.at[my_dp], up_all.at[my_dp], up_s.at[k], up_r.at[k], target)
+        for k, target in enumerate(z_peers)
+    ]
+    start_all(ups)
+    up_twins = [send(up_all.at[my_dp], up_all.at[my_dp], up_ts.at[0], up_tr.at[0], twin)]
+    start_all(up_twins)
+    for copies, onward, whole, send_sem, recv_sem in (
+        (downs, down_twins, down_all, down_ts, down_tr),
+        (ups, up_twins, up_all, up_ts, up_tr),
+    ):
+        for k in range(1, n_z):
+            copies[k - 1].wait_recv()
+            slot = lax.rem(my_z + n_z - k, n_z) * 2 + core
+            onward.append(send(whole.at[slot], whole.at[slot], send_sem.at[k], recv_sem.at[k], twin))
+            onward[-1].start()
+    for copy in downs + ups:
+        copy.wait_send()
+    for copy in down_twins + up_twins + rows:
+        copy.wait()
+
+
+def open_gather(x, dy, up, down):
+    n_seq, n_dp = lax.axis_size("seq"), lax.axis_size("dp")
+    n_z = n_dp // 2
+    sems = [n_seq - 1] * 6 + [n_z - 1] * 4 + [n_z] * 4 + [4]
+    return pl.pallas_call(
+        functools.partial(open_kernel, n_z, n_seq),
+        out_shape=(
+            jax.ShapeDtypeStruct((n_seq, *x.shape), x.dtype),
+            jax.ShapeDtypeStruct((n_seq, *dy.shape), dy.dtype),
+            jax.ShapeDtypeStruct((n_dp, *up.shape), up.dtype),
+            jax.ShapeDtypeStruct((n_dp, *down.shape), down.dtype),
+        ),
+        in_specs=[pl.BlockSpec(memory_space=pl.ANY)] * 4,
+        out_specs=[pl.BlockSpec(memory_space=pl.ANY)] * 4,
+        scratch_shapes=[pltpu.SemaphoreType.DMA((extent,)) for extent in sems],
+        compiler_params=pltpu.CompilerParams(collective_id=0, has_side_effects=True),
+        cost_estimate=pl.CostEstimate(flops=0, bytes_accessed=200_000_000, transcendentals=0),
+        name="open_gather",
+    )(x, dy, up, down)
+
+
+def total_kernel(n_dp, n_seq, values, out, by_seq, part, by_dp, s_send, s_recv, d_send, d_recv):
+    my_dp, my_seq = lax.axis_index("dp"), lax.axis_index("seq")
+    seq_peers = [(my_dp, lax.rem(my_seq + step, n_seq)) for step in range(1, n_seq)]
+    dp_peers = [(lax.rem(my_dp + step, n_dp), my_seq) for step in range(1, n_dp)]
+    greet(seq_peers + dp_peers)
+    copies = [
+        send(values, by_seq.at[k], s_send.at[k], s_recv.at[k], target)
+        for k, target in enumerate(seq_peers)
+    ]
+    start_all(copies)
+    for copy in copies:
+        copy.wait()
+    part[...] = values[...] + jnp.sum(by_seq[...], axis=0)
+    copies = [
+        send(part, by_dp.at[k], d_send.at[k], d_recv.at[k], target)
+        for k, target in enumerate(dp_peers)
+    ]
+    start_all(copies)
+    for copy in copies:
+        copy.wait()
+    out[...] = part[...] + jnp.sum(by_dp[...], axis=0)
+
+
+def total(values, number):
+    n_seq, n_dp = lax.axis_size("seq"), lax.axis_size("dp")
+    return pl.pallas_call(
+        functools.partial(total_kernel, n_dp, n_seq),
+        out_shape=jax.ShapeDtypeStruct(values.shape, values.dtype),
+        in_specs=[pl.BlockSpec(memory_space=pltpu.VMEM)],
+        out_specs=pl.BlockSpec(memory_space=pltpu.VMEM),
+        scratch_shapes=[
+            pltpu.VMEM((n_seq - 1, *values.shape), values.dtype),
+            pltpu.VMEM(values.shape, values.dtype),
+            pltpu.VMEM((n_dp - 1, *values.shape), values.dtype),
+            pltpu.SemaphoreType.DMA((n_seq - 1,)),
+            pltpu.SemaphoreType.DMA((n_seq - 1,)),
+            pltpu.SemaphoreType.DMA((n_dp - 1,)),
+            pltpu.SemaphoreType.DMA((n_dp - 1,)),
+        ],
+        compiler_params=pltpu.CompilerParams(collective_id=number, has_side_effects=True),
+        cost_estimate=pl.CostEstimate(flops=0, bytes_accessed=40_000_000, transcendentals=0),
+        name=f"total_{number}",
+    )(values)
+
+
+def gather_seq(rows, number):
+    return exchange(rows, number, True).reshape(-1, rows.shape[-1])
+
+
+def scatter_seq(rows, number):
+    count = lax.axis_size("seq")
+    chunks = exchange(rows.reshape(count, -1, rows.shape[-1]), number, False)
+    return jnp.sum(chunks.astype(wide), axis=0)
+
+
+def late_scatter_seq(rows):
     return lax.psum_scatter(rows, "seq", scatter_dimension=0, tiled=True).astype(wide)
 
 
@@ -124,19 +324,22 @@
     ff_bias = ff_bias.astype(wide)
 
     part_qkv = qkv_weight.reshape(w_rows, 3, n_seq, cols).transpose(2, 0, 1, 3)
-    part_qkv = swap_seq(part_qkv.reshape(n_seq, w_rows, 3 * cols))
-    w_qkv = gather_dp(part_qkv.reshape(n_seq * w_rows, 3 * cols))
+    part_fc1 = fc1_weight.reshape(w_rows, n_dp, n_seq, ff_rows).transpose(2, 0, 1, 3)
+    up = jnp.concatenate(
+        [part_qkv.reshape(n_seq, w_rows, 3 * cols), part_fc1.reshape(n_seq, w_rows, units)], axis=2
+    )
     w_dense = gather_dp(lax.ppermute(dense_weight, ("dp", "seq"), spread))
-    part_fc1 = fc1_weight.reshape(w_rows, n_dp, n_seq, ff_rows).transpose(2, 0, 1, 3)
-    part_fc1 = swap_seq(part_fc1.reshape(n_seq, w_rows, units))
-    w_fc1 = gather_dp(part_fc1.reshape(n_seq * w_rows, units))
-    w_fc2 = gather_dp(fc2_weight)
+    dy = out_grad[0]
+    x_all, dy_all, up_all, w_fc2 = open_gather(tokens[0], dy, up, fc2_weight)
+    up_all = up_all.reshape(width, 3 * cols + units)
+    w_qkv, w_fc1 = up_all[:, : 3 * cols], up_all[:, 3 * cols :]
+    w_fc2 = w_fc2.reshape(units, width)
+    dy_all = dy_all.reshape(length, width)
 
     inputs = tokens[0].astype(wide)
-    normed_one, norm_pull_one = jax.vjp(layer_norm, inputs, gains[0], shifts[0])
-    h_one = gather_seq(normed_one.astype(low))
-    dy = out_grad[0]
-    dy_all = gather_seq(dy)
+    _, norm_pull_one = jax.vjp(layer_norm, inputs, gains[0], shifts[0])
+    x_all = x_all.reshape(length, width).astype(wide)
+    h_one = layer_norm(x_all, gains[0], shifts[0]).astype(low)
 
     def my_cols(row):
         return lax.dynamic_slice_in_dim(row, my_seq * cols, cols, 0)
@@ -148,18 +351,18 @@
     slopes = lax.dynamic_slice_in_dim(alibi_slopes, my_seq * local_heads, local_heads, 0)
     attended, kept = attention_forward(q_heads, k_heads, v_heads, slopes, block)
     attended_low = attended.astype(low).transpose(1, 0, 2).reshape(length, cols)
-    branch = scatter_seq(dot("tc,cd->td", attended_low, w_dense).astype(low))
+    branch = scatter_seq(dot("tc,cd->td", attended_low, w_dense).astype(low), 1)
     residual = inputs + branch + shifts[3]
     normed_two, norm_pull_two = jax.vjp(layer_norm, residual, gains[1], shifts[4])
-    h_two = gather_seq(normed_two.astype(low))
+    h_two = gather_seq(normed_two.astype(low), 2)
     upper = dot("td,df->tf", h_two, w_fc1) + ff_bias
     activated, gelu_pull = jax.vjp(gelu_tanh, upper)
     act_low = activated.astype(low)
     grad_act = dot("td,fd->tf", dy_all, w_fc2)
     grad_upper = gelu_pull(grad_act)[0].astype(low)
-    grad_h_two = scatter_seq(dot("tf,df->td", grad_upper, w_fc1).astype(low))
+    grad_h_two = scatter_seq(dot("tf,df->td", grad_upper, w_fc1).astype(low), 3)
     layer_out = (
-        residual + scatter_seq(dot("tf,fd->td", act_low, w_fc2).astype(low)) + shifts[5]
+        residual + late_scatter_seq(dot("tf,fd->td", act_low, w_fc2).astype(low)) + shifts[5]
     ).astype(low)
     grad_fc2 = scatter_dp(dot("tf,td->fd", act_low, dy_all).astype(low))
     grad_fc1 = scatter_dp(dot("td,tf->df", h_two, grad_upper).astype(low))
@@ -168,7 +371,7 @@
     grad_res_norm, grad_gain_two, grad_shift_two = norm_pull_two(grad_h_two)
     grad_resid = dy.astype(wide) + grad_res_norm
     grad_branch = grad_resid.astype(low)
-    branch_all = gather_seq(grad_branch)
+    branch_all = gather_seq(grad_branch, 4)
     grad_dense = scatter_dp(dot("tc,td->cd", attended_low, branch_all).astype(low))
     grad_attended = dot("td,cd->tc", branch_all, w_dense).astype(low)
     g_heads = grad_attended.reshape(length, local_heads, HEAD_DIM).transpose(1, 0, 2)
@@ -178,7 +381,7 @@
     )
     grad_proj = jnp.stack([grad_q, grad_k, grad_v]).astype(low)
     grad_proj = grad_proj.transpose(2, 0, 1, 3).reshape(length, 3 * cols)
-    grad_h_one = scatter_seq(dot("tc,dc->td", grad_proj, w_qkv).astype(low))
+    grad_h_one = scatter_seq(dot("tc,dc->td", grad_proj, w_qkv).astype(low), 5)
     grad_qkv = scatter_dp(dot("td,tc->dc", h_one, grad_proj).astype(low))
     proj_sums = jnp.sum(grad_proj, axis=0, dtype=wide)
 
@@ -205,7 +408,8 @@
             jnp.sum(dy, axis=0, dtype=wide),
         ]
     )
-    sums = lax.psum(jnp.concatenate([vec_sums.reshape(-1), ff_placed.reshape(-1)]), ("dp", "seq"))
+    sums = jnp.concatenate([vec_sums.reshape(-1, 128), ff_placed.reshape(-1, 128)])
+    sums = total(sums, 6).reshape(-1)
     vec_sums = lax.dynamic_slice_in_dim(sums[: 8 * width].reshape(8, width), me * w_rows, w_rows, 1)
     fc1_bias_grad = lax.dynamic_slice_in_dim(sums, 8 * width + me * ff_rows, ff_rows, 0)
 

time: 696 us -> 528 us (0.76)
  waiting for transfers between devices: 382 us -> 24.4 us
  Pallas kernels: 0 us -> 230 us
  blocking collectives: 141 us -> 90.4 us
  other arithmetic: 31.6 us -> 41 us
  matrix products: 87.4 us -> 78.3 us
    pallas_call x0 -> x7, Pallas kernels: none -> 230 us  [the longest x5 135 us: exchange(): pl.pallas_call(functools.partial(exchange_kernel, count, is_gather), out_...]
    all_gather x7 -> x0, waiting for transfers between devices: 154 us -> none  [the longest x4 98.8 us: gather_seq(): return lax.all_gather(rows, 'seq', axis=0, tiled=True)]
    reduce_scatter x4 -> x1, waiting for transfers between devices: 121 us -> 0.42 us  [late_scatter_seq(): lax.psum_scatter(rows, 'seq', scatter_dimension=0, tiled=True).astype(wide)]
    reduce_scatter x4, waiting for transfers between devices: 106 us -> 23.9 us  [scatter_dp(): return lax.psum_scatter(rows, 'dp', scatter_dimension=0, tiled=True)]
    psum x1 -> x0, blocking collectives: 39.8 us -> none  [body(): lax.psum(jnp.concatenate([vec_sums.reshape(-1), ff_placed.reshape(-1)]),...]
    all_to_all x2 -> x0, blocking collectives: 21.1 us -> none  [swap_seq(): lax.all_to_all(chunks, 'seq', split_axis=0, concat_axis=0, tiled=True)]
    dot_general x32, matrix products: 70.9 us -> 61.7 us  [dot(): return jnp.einsum(spec, left, right, preferred_element_type=wide)]
  transfers between devices with their start and end apart: 19 -> 9, of which waited for: 14 -> 2; matrix products, arithmetic and copies ran while one was open for 10% -> 23% of each run, Pallas kernels for 0% -> 34%
where the time goes in v2:
time: 528 us; the launch traced here: 518 us
  Pallas kernels  230 us (44%)
  blocking collectives  90.4 us (17%)
  matrix products  78.3 us (15%)
  other arithmetic  41 us (8%)
  local copies, waits for them, and re-layouts  27 us (5%)
  waiting for transfers between devices  24.4 us (5%)
  between operations  15.2 us (3%)
  starting transfers between devices  11.6 us (2%)
    pallas_call x5, Pallas kernels, exchange(): pl.pallas_call(functools.partial(exchange_kernel, count, is_gather), out_...  135 us
    pallas_call x1, Pallas kernels, open_gather(): pl.pallas_call(functools.partial(open_kernel, n_z, n_seq), out_shape=(jax...  78.2 us
    all_gather x1, blocking collectives, body(): small = lax.all_gather(small, ('dp', 'seq'), axis=0, tiled=False)  69.9 us
    dot_general x32, matrix products, dot(): return jnp.einsum(spec, left, right, preferred_element_type=wide)  61.7 us
    reduce_scatter x4, waiting for transfers between devices, scatter_dp(): return lax.psum_scatter(rows, 'dp', scatter_dimension=0, tiled=True)  23.9 us
    all_gather x1, blocking collectives, gather_dp(): return lax.all_gather(rows, 'dp', axis=0, tiled=True)  20.6 us
    pallas_call x1, Pallas kernels, total(): pl.pallas_call(functools.partial(total_kernel, n_dp, n_seq), out_shape=ja...  17.6 us
    sub x4, matrix products, attention_forward(): weights = jnp.exp(scores - jnp.max(scores, axis=-1, keepdims=True))  16.7 us
  transfers between devices with their start and end apart: 9, of which 2 were waited for; matrix products, arithmetic and copies ran while one was open for 23% of the time, Pallas kernels for 34%

profile of v2, /device:TPU:0, one launch (start us, length us, event | category | flops | bytes accessed | tf_op | source)
XLA Modules:
  0.0 518.3 jit_solution(8745989429709511473)
XLA Ops:
  11.7 69.9 %all-gather.1 = bf16[32,1,384]{2,1,0:T(2,128)(2,1)S(1)} all-gather(bf16[1,1,384]{2,1,0:T(2,128)(2,1)S(1)} %reshape.811), channel_id=2, replica_groups=mesh['dp'=8,'seq'=4] {'dp','seq'}, dimensions={0}, use_global_device_ids=true | all-gather | bytes 25344 | tf_op jit(solution)/shard_map/all_gather | solution.py:318
  91.7 78.2 %open_gather.1 = (bf16[4,256,1024]{2,1,0:T(8,128)(2,1)}, bf16[4,256,1024]{2,1,0:T(8,128)(2,1)}, bf16[8,4,32,1792]{3,2,1,0:T(8,128)(2,1)}, bf16[8,128,1024]{2,1,0:T(8,128)(2,1)}) custom-call(bf16[256,1024]{1,0:T(8,128)(2,1)} %bitcast.157, bf16[256,1024]{1,0:T(8,128)(2,1)} %bitcast.159, bf16[4,32,1792]{2,1,0:T(8,128)(2,1)} %pad_maximum_fusion.2.up, ...), custom_call_target="tpu_custom_call" | custom-call | bytes 200000000 | tf_op jit(solution)/shard_map/open_gather/pallas_call | solution.py:163
  174.3 3.3 add_convert_fusion.1
  184.7 3.5 fusion.166
  192.8 4.4 fusion.161
  201.9 5.7 %fusion.158 = (f32[4,256]{1,0:T(4,128)S(1)}, f32[4,256,1024]{2,1,0:T(8,128)}) fusion(f32[256,1024]{1,0:T(8,128)} %subtract_convert_fusion, f32[4]{0:T(128)S(1)} %copy-done.47, pred[256,1024]{1,0:T(8,128)(4,1)} %broadcast_compare_fusion, bf16[4,1024,64]{1,2,0:T(8,128)(2,1)S(1)} %get-tuple-element.159, bf16[3,4,1024,64]{2,3,1,0:T(8,128)(2,1)} %bitcast.161), kind=kOutput, calls=%fused_computation.254 | convolution fusion | flops 140510208 | bytes 6164992 | tf_op jit(solution)/shard_map/sub | solution.py:262
  213.5 20.6 %all_gather.11 = bf16[256,1024]{1,0:T(8,128)(2,1)S(1)} all-gather(bf16[32,1024]{1,0:T(8,128)(2,1)} %collective-permute-done), channel_id=1, replica_groups=mesh['dp'=8,'seq'=4] {'dp'}, dimensions={0}, use_global_device_ids=true | all-gather | bytes 589824 | tf_op jit(solution)/shard_map/all_gather | solution.py:244
  236.2 26.7 %exchange_1.1 = bf16[4,256,1024]{2,1,0:T(8,128)(2,1)} custom-call(bf16[4,256,1024]{2,1,0:T(8,128)(2,1)} %bitcast.158), custom_call_target="tpu_custom_call" | custom-call | bytes 60000000 | tf_op jit(solution)/shard_map/exchange_1/pallas_call | solution.py:82
  267.3 26.4 %exchange_2.1 = bf16[4,256,1024]{2,1,0:T(8,128)(2,1)} custom-call(bf16[256,1024]{1,0:T(8,128)(2,1)} %add_convert_fusion.3.src), custom_call_target="tpu_custom_call" | custom-call | bytes 60000000 | tf_op jit(solution)/shard_map/exchange_2/pallas_call | solution.py:82
  293.7 4.7 fusion.23
  300.4 4.1 convolution_convert_fusion.3
  308.3 6.9 %convert_reduce_fusion.4 = (f32[1024]{0:T(1024)S(1)}, bf16[1024,1024]{1,0:T(8,128)(2,1)S(1)}) fusion(f32[1024,1024]{1,0:T(8,128)} %copy-done.48, f32[1024]{0:T(1024)S(1)} %bitcast.208, bf16[1024,1024]{1,0:T(8,128)(2,1)S(1)} %bitcast.217, bf16[1024,1024]{1,0:T(8,128)(2,1)S(1)} %bitcast.219), kind=kOutput, calls=%fused_computation.22 | convolution fusion | flops 2171599872 | bytes 10493952 | tf_op jit(solution)/shard_map/td,fd->tf/dot_general | solution.py:31
  315.2 3.7 convolution_convert_fusion.2
  318.9 28.8 %exchange_3.1 = bf16[4,256,1024]{2,1,0:T(8,128)(2,1)} custom-call(bf16[4,256,1024]{2,1,0:T(8,128)(2,1)} %bitcast.172), custom_call_target="tpu_custom_call" | custom-call | bytes 60000000 | tf_op jit(solution)/shard_map/exchange_3/pallas_call | solution.py:82
  350.9 3.7 convolution_convert_fusion.1
  358.7 26.2 %exchange_4.1 = bf16[4,256,1024]{2,1,0:T(8,128)(2,1)} custom-call(bf16[256,1024]{1,0:T(8,128)(2,1)} %get-tuple-element.148.src), custom_call_target="tpu_custom_call" | custom-call | bytes 60000000 | tf_op jit(solution)/shard_map/exchange_4/pallas_call | solution.py:82
  402.7 3.1 convolution_convert_fusion.7
  406.1 7.4 %convolution_convert_fusion = bf16[1024,1024]{1,0:T(8,128)(2,1)} fusion(bf16[1024,1024]{1,0:T(8,128)(2,1)} %bitcast.216, f32[1024,1024]{1,0:T(8,128)} %copy-done.48, f32[1024]{0:T(1024)S(1)} %bitcast.209), kind=kOutput, calls=%fused_computation.49 | convolution fusion | flops 2159017984 | bytes 8392704 | tf_op jit(solution)/shard_map/tf,td->fd/dot_general | solution.py:31
  413.6 3.4 all-to-all-start.1
  417.0 5.1 convolution_convert_fusion.5
  422.1 26.6 %exchange_5.1 = bf16[4,256,1024]{2,1,0:T(8,128)(2,1)} custom-call(bf16[4,256,1024]{2,1,0:T(8,128)(2,1)} %bitcast.171), custom_call_target="tpu_custom_call" | custom-call | bytes 60000000 | tf_op jit(solution)/shard_map/exchange_5/pallas_call | solution.py:82
  455.5 3.6 all-to-all-start
  459.8 17.6 %total_6.1 = f32[96,128]{1,0:T(8,128)} custom-call(f32[96,128]{1,0:T(8,128)} %pad_maximum_fusion.3.values), custom_call_target="tpu_custom_call" | custom-call | bytes 40000000 | tf_op jit(solution)/shard_map/total_6/pallas_call | solution.py:205
  482.2 23.8 %reduce-scatter.14.cloned.1.call-done = bf16[128,1024]{1,0:T(8,128)(2,1)} async-done(((bf16[1024,1024]{1,0:T(8,128)(2,1)}), bf16[128,1024]{1,0:T(8,128)(2,1)}) %reduce-scatter.14.cloned.1.call-update) | async-done | bytes 262160 | tf_op jit(solution)/shard_map/reduce_scatter | solution.py:248
  (254 shorter events, 95.9 us)
Async XLA Ops:
  7.2 82.9 %copy-start.36 = (bf16[32,3072]{1,0:T(8,128)(2,1)S(1)}, bf16[32,3072]{1,0:T(8,128)(2,1)}, u32[]{:S(2)}) copy-start(bf16[32,3072]{1,0:T(8,128)(2,1)} %param.33) | copy-start | bytes 589828
  7.2 348.2 %reduce-scatter.6.cloned.1.call-start = ((), (), s32[]{:S(2)}) async-start(), calls=%async_computation.7 | async-start | bytes 2621440 | tf_op jit(solution)/shard_map/reduce_scatter | solution.py:236
  7.2 206.2 %collective-permute-start = (bf16[32,1024]{1,0:T(8,128)(2,1)}, bf16[32,1024]{1,0:T(8,128)(2,1)}, u32[]{:S(2)}, u32[]{:S(2)}) collective-permute-start(bf16[32,1024]{1,0:T(8,128)(2,1)} %param.34), channel_id=1, source_target_pairs={{0,0},{1,4},{2,8},{3,12},{4,16},{5,20},{6,24},{7,28},{8,1},{9,5},{... | collective-permute-start | bytes 196616 | tf_op jit(solution)/shard_map/ppermute | solution.py:331
  84.0 6.5 %copy-start.35 = (bf16[32,4096]{1,0:T(8,128)(2,1)S(1)}, bf16[32,4096]{1,0:T(8,128)(2,1)}, u32[]{:S(2)}) copy-start(bf16[32,4096]{1,0:T(8,128)(2,1)} %param.35) | copy-start | bytes 786436
  89.3 84.2 %copy-start.38 = (f32[1024]{0:T(1024)}, f32[1024]{0:T(1024)S(1)}, u32[]{:S(2)}) copy-start(f32[1024]{0:T(1024)S(1)} %add.249) | copy-start | bytes 12292
  179.7 19.7 %copy-start.14 = (bf16[4,1024,64]{1,2,0:T(8,128)(2,1)}, bf16[4,1024,64]{1,2,0:T(8,128)(2,1)S(1)}, u32[]{:S(2)}) copy-start(bf16[4,1024,64]{1,2,0:T(8,128)(2,1)S(1)} %get-tuple-element.157) | copy-start | bytes 1572868
  179.7 22.1 %copy-start.25 = (bf16[4,1024,64]{1,2,0:T(8,128)(2,1)}, bf16[4,1024,64]{1,2,0:T(8,128)(2,1)S(1)}, u32[]{:S(2)}) copy-start(bf16[4,1024,64]{1,2,0:T(8,128)(2,1)S(1)} %get-tuple-element.159) | copy-start | bytes 1572868
  213.3 22.8 %copy-start.33 = (f32[4,256,64]{1,2,0:T(8,128)}, f32[4,256,64]{1,2,0:T(8,128)S(1)}, u32[]{:S(2)}) copy-start(f32[4,256,64]{1,2,0:T(8,128)S(1)} %fusion.150) | copy-start | bytes 786436
  213.4 20.6 %copy-start.21 = (bf16[4,1024,64]{1,2,0:T(8,128)(2,1)}, bf16[4,1024,64]{1,2,0:T(8,128)(2,1)S(1)}, u32[]{:S(2)}) copy-start(bf16[4,1024,64]{1,2,0:T(8,128)(2,1)S(1)} %fusion.71) | copy-start | bytes 1572868
  293.7 6.6 %copy-start.45 = (bf16[8,128,1024]{2,1,0:T(8,128)(2,1)S(1)}, bf16[8,128,1024]{2,1,0:T(8,128)(2,1)}, u32[]{:S(2)}) copy-start(bf16[8,128,1024]{2,1,0:T(8,128)(2,1)} %get-tuple-element.127) | copy-start | bytes 6291460
  304.5 109.1 %reduce-scatter.12.cloned.1.call-start = ((), (), s32[]{:S(2)}) async-start(), calls=%async_computation.10 | async-start | bytes 2359296 | tf_op jit(solution)/shard_map/reduce_scatter | solution.py:248
  308.3 6.9 %copy-start.43 = (bf16[8,4,32,1792]{3,2,1,0:T(8,128)(2,1)S(1)}, bf16[8,4,32,1792]{3,2,1,0:T(8,128)(2,1)}, u32[]{:S(2)}) copy-start(bf16[8,4,32,1792]{3,2,1,0:T(8,128)(2,1)} %get-tuple-element.126) | copy-start | bytes 11010052
  315.1 3.7 copy-start.49
  347.7 3.2 copy-start.18
  354.7 100.8 %reduce-scatter.8.cloned.1.call-start = ((), (), s32[]{:S(2)}) async-start(), calls=%async_computation.8 | async-start | bytes 1769472 | tf_op jit(solution)/shard_map/reduce_scatter | solution.py:248
  357.6 27.3 %copy-start.24 = (bf16[256,1024]{1,0:T(8,128)(2,1)S(1)}, bf16[256,1024]{1,0:T(8,128)(2,1)}, u32[]{:S(2)}) copy-start(bf16[256,1024]{1,0:T(8,128)(2,1)} %copy-done.23) | copy-start | bytes 1572868
  357.7 27.3 %copy-start.30 = (f32[4,256,64]{1,2,0:T(8,128)S(1)}, f32[4,256,64]{1,2,0:T(8,128)}, u32[]{:S(2)}) copy-start(f32[4,256,64]{1,2,0:T(8,128)} %fusion.76) | copy-start | bytes 786436
  357.7 27.3 %copy-start.32 = (f32[4,256,64]{1,2,0:T(8,128)S(1)}, f32[4,256,64]{1,2,0:T(8,128)}, u32[]{:S(2)}) copy-start(f32[4,256,64]{1,2,0:T(8,128)} %fusion.86) | copy-start | bytes 786436
  357.7 27.3 %copy-start.34 = (f32[4,256,64]{1,2,0:T(8,128)S(1)}, f32[4,256,64]{1,2,0:T(8,128)}, u32[]{:S(2)}) copy-start(f32[4,256,64]{1,2,0:T(8,128)} %copy-done.33) | copy-start | bytes 786436
  402.6 75.6 %reduce-scatter.10.cloned.1.call-start = ((), (), s32[]{:S(2)}) async-start(), calls=%async_computation.9 | async-start | bytes 589824 | tf_op jit(solution)/shard_map/reduce_scatter | solution.py:248
  405.8 100.2 %reduce-scatter.14.cloned.1.call-start = ((), (), s32[]{:S(2)}) async-start(), calls=%async_computation.11 | async-start | bytes 2359296 | tf_op jit(solution)/shard_map/reduce_scatter | solution.py:248
  413.6 41.9 %all-to-all-start.1 = ((bf16[4,32,1024]{2,1,0:T(8,128)(2,1)}), bf16[4,32,1024]{2,1,0:T(8,128)(2,1)S(1)}, u32[]{:S(2)}, u32[]{:S(2)}) async-start(bf16[4,32,1024]{2,1,0:T(8,128)(2,1)} %bitcast.191), calls=%async_computation.5 | async-start | bytes 524288 | tf_op jit(solution)/shard_map/all_to_all | solution.py:240
  455.5 54.3 %all-to-all-start = ((bf16[4,32,768]{2,1,0:T(8,128)(2,1)}), bf16[4,32,768]{2,1,0:T(8,128)(2,1)S(1)}, u32[]{:S(2)}, u32[]{:S(2)}) async-start(bf16[4,32,768]{2,1,0:T(8,128)(2,1)} %bitcast.192), calls=%async_computation.2 | async-start | bytes 393216 | tf_op jit(solution)/shard_map/all_to_all | solution.py:240
  478.2 31.0 %collective-permute-start.1 = (bf16[32,1024]{1,0:T(8,128)(2,1)}, bf16[32,1024]{1,0:T(8,128)(2,1)S(1)}, u32[]{:S(2)}, u32[]{:S(2)}) collective-permute-start(bf16[32,1024]{1,0:T(8,128)(2,1)} %reduce-scatter.10.cloned.1.call-done), channel_id=1, source_target_pairs={{0,0},{4,1},{8,2},{12,3},{16,4},{20,5},{24,6},{28,7},{1,8},{5,9},{... | collective-permute-start | bytes 196616 | tf_op jit(solution)/shard_map/ppermute | solution.py:420
  (36 other events, 64.8 us)
Sparse Core Ops, SparseCore 0:
  304.6 50.6 reduce-scatter.5
  357.8 35.6 reduce-scatter.11
  402.7 33.9 reduce-scatter.7
  439.5 29.1 reduce-scatter.9
  470.8 35.1 reduce-scatter.13
